TPU v7x, 512 devices: a whole 4x8x8 slice. The times are simulated.
512 devices in a mesh: pool: 2 (over y_lo), wide: 64 (over z, x, core), narrow: 4 (over y_hi).
Axes of the slice: x: 4, y: 8 (y_hi: 4, y_lo: 2; y = y_hi * 2 + y_lo), z: 8, core: 2. Of those that a mesh axis runs over, the one named last changes fastest.
Arguments:
- queries: bfloat16 [128, 64, 128], P('wide', 'narrow'), may hold values from -160 to 160
- new_keys: bfloat16 [128, 4, 128], P('wide', 'narrow'), may hold values from -6 to 6
- new_values: bfloat16 [128, 4, 128], P('wide', 'narrow'), may hold values from -6 to 6
- key_cache: bfloat16 [128, 512, 4, 128], P('wide', None, 'narrow'), may hold values from -6 to 6
- value_cache: bfloat16 [128, 512, 4, 128], P('wide', None, 'narrow'), may hold values from -6 to 6
- lengths: int32 [128], P('wide'), may hold values from 8 to 512, as said below
- residual: bfloat16 [128, 2048], P(None, 'wide'), may hold values from -3 to 3
- out_weight: bfloat16 [2048, 8192], P('wide', 'narrow'), may hold values from -0.125 to 0.125
- norm_gain: bfloat16 [2048], replicated, may hold values from 0.099609375 to 1.8984375
- expert_ids: int32 [128, 8], replicated, may hold values from 0 to 63, all different within a row; in each aligned block of 128 rows (0 to 127, 128 to 255, ...) at most 32 rows name the same one
- expert_weights: float32 [128, 8], replicated, may hold values from 0.05 to 1
- gate_proj: bfloat16 [64, 768, 2048], P('wide', 'narrow'), may hold values from -0.125 to 0.125
- up_proj: bfloat16 [64, 768, 2048], P('wide', 'narrow'), may hold values from -0.125 to 0.125
- down_proj: bfloat16 [64, 768, 2048], P('wide', 'narrow'), may hold values from -0.3125 to 0.3125
Outputs:
- mixed: bfloat16 [128, 2048], P(('pool', 'narrow'), 'wide')
Inputs may be any that keep to these rules, and one draw needn't show every extreme that they name: `lengths`: at least one row has all 512 slots filled. `expert_ids`: the 8 experts of a row differ. Over all 128 rows no expert is named by more than 32 rows, a bound that some block reaches.
All inputs are finite; a program needn't handle non-finite values.
Results may differ from a plain program's by a relative error of at most 0.018.
Values may be sent and summed in bfloat16 or wider, within the bound.
A program may use at most 64 MiB of HBM per device.

v0:
```python
import jax
import jax.numpy as jnp
from jax import lax
from jax.sharding import PartitionSpec as P


def attend(queries, new_keys, new_values, key_cache, value_cache, lengths):
    scale = 1.0 / queries.shape[2] ** 0.5
    keys = key_cache[:, :, 0, :]
    values = value_cache[:, :, 0, :]
    scores = jnp.einsum("rgd,rcd->rgc", queries, keys, preferred_element_type=jnp.float32) * scale
    self_score = (
        jnp.einsum("rgd,rd->rg", queries, new_keys[:, 0, :], preferred_element_type=jnp.float32)
        * scale
    )
    positions = jnp.arange(keys.shape[1], dtype=jnp.int32)
    valid = (positions[None, :] < lengths[:, None])[:, None, :]
    scores = jnp.where(valid, scores, -1e30)
    peak = jnp.maximum(jnp.max(scores, axis=-1), self_score)
    weights = jnp.where(valid, jnp.exp(scores - peak[..., None]), 0.0)
    self_weight = jnp.exp(self_score - peak)
    total = jnp.sum(weights, axis=-1) + self_weight
    probs = (weights / total[..., None]).astype(jnp.bfloat16)
    self_prob = (self_weight / total).astype(jnp.bfloat16)
    mixed = jnp.einsum("rgc,rcd->rgd", probs, values, preferred_element_type=jnp.float32)
    mixed = (
        mixed
        + self_prob.astype(jnp.float32)[..., None]
        * new_values[:, 0, :].astype(jnp.float32)[:, None, :]
    )
    return mixed.astype(jnp.bfloat16).reshape(queries.shape[0], -1)


def local(
    queries,
    new_keys,
    new_values,
    key_cache,
    value_cache,
    lengths,
    residual,
    out_weight,
    norm_gain,
    expert_ids,
    expert_weights,
    gate_proj,
    up_proj,
    down_proj,
):
    wide_count = lax.axis_size("wide")
    on_attention = lax.axis_index("pool") == 0
    on_experts = lax.axis_index("pool") == 1
    owner = lax.axis_index("wide")
    width_cols = out_weight.shape[0]
    model_width = width_cols * wide_count
    total_rows = expert_ids.shape[0]
    topk = expert_ids.shape[1]
    expert_count = gate_proj.shape[0] * wide_count
    capacity = 2 * total_rows * topk // expert_count
    heads_local = lax.cond(
        on_attention,
        lambda: attend(queries, new_keys, new_values, key_cache, value_cache, lengths),
        lambda: jnp.zeros((queries.shape[0], queries.shape[1] * queries.shape[2]), jnp.bfloat16),
    )
    group_part = jnp.einsum(
        "rk,ck->rc",
        lax.all_gather(heads_local, "wide", axis=0, tiled=True),
        out_weight,
        preferred_element_type=jnp.float32,
    ).astype(jnp.bfloat16)
    expert_range = jnp.arange(expert_count, dtype=jnp.int32)
    hits = jnp.sum((expert_ids[:, :, None] == expert_range).astype(jnp.int32), axis=1)
    slots = jnp.cumsum(hits, axis=0) - 1
    slot_range = jnp.arange(capacity, dtype=jnp.int32)
    table = jnp.where(
        (slots.T[:, None, :] == slot_range[None, :, None]) & (hits.T[:, None, :] > 0), 1.0, 0.0
    ).astype(jnp.bfloat16)
    send_part = jnp.einsum(
        "ecr,rk->eck", table, group_part, preferred_element_type=jnp.float32
    ).astype(jnp.bfloat16)
    send_resid = jnp.einsum(
        "ecr,rk->eck", table, residual, preferred_element_type=jnp.float32
    ).astype(jnp.bfloat16)
    blank = jnp.zeros_like(send_part)
    arrived_part, arrived_resid = (
        lax.all_to_all(
            jnp.concatenate([blank, send_part], axis=0),
            ("pool", "wide"),
            split_axis=0,
            concat_axis=2,
            tiled=True,
        ),
        lax.all_to_all(
            jnp.concatenate([blank, send_resid], axis=0),
            ("pool", "wide"),
            split_axis=0,
            concat_axis=2,
            tiled=True,
        ),
    )
    arrived_part = arrived_part[0, :, :model_width]
    arrived_resid = arrived_resid[0, :, :model_width]
    summed = lax.psum(arrived_part.astype(jnp.float32).astype(jnp.bfloat16), "narrow").astype(
        jnp.float32
    )
    hidden_rows = arrived_resid.astype(jnp.float32) + summed
    shares = expert_weights / jnp.sum(expert_weights, axis=-1, keepdims=True)
    row_share = jnp.sum(jnp.where(expert_ids == owner, shares, 0.0), axis=-1)
    own_table = lax.dynamic_index_in_dim(table, owner, 0, keepdims=False)
    slot_share = jnp.dot(own_table.astype(jnp.float32), row_share, precision=lax.Precision.HIGHEST)

    def experts_work():
        normed = (
            hidden_rows
            * lax.rsqrt(jnp.mean(hidden_rows * hidden_rows, axis=-1, keepdims=True) + 1e-06)
            * norm_gain.astype(jnp.float32)
        ).astype(jnp.bfloat16)
        gate_vals = jnp.einsum(
            "cd,fd->cf", normed, gate_proj[0], preferred_element_type=jnp.float32
        )
        up_vals = jnp.einsum("cd,fd->cf", normed, up_proj[0], preferred_element_type=jnp.float32)
        activated = (jax.nn.silu(gate_vals) * up_vals).astype(jnp.bfloat16)
        down_split = down_proj[0].reshape(down_proj.shape[1], wide_count, width_cols)
        output = jnp.einsum(
            "cf,fwk->wck", activated, down_split, preferred_element_type=jnp.float32
        )
        return (output * slot_share[None, :, None]).astype(jnp.bfloat16)

    produced = lax.cond(
        on_experts,
        experts_work,
        lambda: jnp.zeros((wide_count, capacity, width_cols), jnp.bfloat16),
    )
    returned = lax.all_to_all(
        jnp.concatenate([produced, jnp.zeros_like(produced)], axis=0),
        ("pool", "wide"),
        split_axis=0,
        concat_axis=0,
        tiled=True,
    )
    returned = returned[wide_count:]
    expert_term = jnp.einsum("ecr,eck->rk", table, returned, preferred_element_type=jnp.float32)
    row_terms = jnp.where(on_attention, group_part.astype(jnp.float32) + expert_term, 0.0)
    share_rows = lax.psum_scatter(row_terms, ("pool", "narrow"), scatter_dimension=0, tiled=True)
    block_rows = share_rows.shape[0]
    block_index = lax.axis_index(("pool", "narrow"))
    resid_rows = lax.dynamic_slice_in_dim(residual, block_index * block_rows, block_rows, 0)
    return (share_rows + resid_rows.astype(jnp.float32)).astype(jnp.bfloat16)


def solution(mesh):
    in_specs = (
        P("wide", "narrow", None),
        P("wide", "narrow", None),
        P("wide", "narrow", None),
        P("wide", None, "narrow", None),
        P("wide", None, "narrow", None),
        P("wide"),
        P(None, "wide"),
        P("wide", "narrow"),
        P(),
        P(),
        P(),
        P("wide", "narrow", None),
        P("wide", "narrow", None),
        P("wide", "narrow", None),
    )
    out_specs = P(("pool", "narrow"), "wide")
    return jax.shard_map(local, mesh=mesh, in_specs=in_specs, out_specs=out_specs, check_vma=False)
```

profile of v0, /device:TPU:12, one launch (start us, length us, event | category | flops | bytes accessed | tf_op | source)
XLA Modules:
  0.0 233.8 jit_solution(9690361058617308389)
XLA Ops:
  6.5 0.8 convert_reduce_fusion
  7.8 0.5 copy-done.5
  8.5 55.9 %all-gather = bf16[64,2,2048]{2,1,0:T(2,128)(2,1)S(1)} all-gather(bf16[1,2,2048]{2,1,0:T(2,128)(2,1)S(1)} %bitcast.93), channel_id=1, replica_groups=mesh['pool'=2,'wide'=64,'narrow'=4] {'wide'}, dimensions={0}, use_global_device_ids=true | all-gather | bytes 532480 | tf_op jit(solution)/shard_map/all_gather | solution.py:67
  65.4 1.5 reshape.56
  66.9 8.4 %all-to-all-start.1 = ((bf16[128,2,512]{2,1,0:T(2,128)(2,1)}), bf16[128,2,512]{2,1,0:T(2,128)(2,1)S(1)}, u32[]{:S(2)}, u32[]{:S(2)}) async-start(bf16[128,2,512]{2,1,0:T(2,128)(2,1)} %reshape.56), calls=%async_computation.1 | async-start | bytes 524288 | tf_op jit(solution)/shard_map/all_to_all | solution.py:86
  75.8 1.5 reshape.54
  77.4 1.1 select_convert_fusion
  78.4 6.6 %all-to-all-done.1 = bf16[128,2,512]{2,1,0:T(2,128)(2,1)S(1)} async-done(((bf16[128,2,512]{2,1,0:T(2,128)(2,1)}), bf16[128,2,512]{2,1,0:T(2,128)(2,1)S(1)}, u32[]{:S(2)}, u32[]{:S(2)}) %all-to-all-start.1) | async-done | bytes 262176 | tf_op jit(solution)/shard_map/all_to_all | solution.py:86
  85.0 9.9 %all-to-all-start = ((bf16[128,2,512]{2,1,0:T(2,128)(2,1)}), bf16[128,2,512]{2,1,0:T(2,128)(2,1)S(1)}, u32[]{:S(2)}, u32[]{:S(2)}) async-start(bf16[128,2,512]{2,1,0:T(2,128)(2,1)} %reshape.54), calls=%async_computation | async-start | bytes 524288 | tf_op jit(solution)/shard_map/all_to_all | solution.py:93
  95.2 0.5 reshape.57
  95.7 0.4 copy.68
  96.1 1.2 all_to_all.36
  97.3 0.7 slice_bitcast_fusion.1
  98.0 0.9 convolution_bitcast_fusion.1
  98.9 5.7 %all-to-all-done = bf16[128,2,512]{2,1,0:T(2,128)(2,1)S(1)} async-done(((bf16[128,2,512]{2,1,0:T(2,128)(2,1)}), bf16[128,2,512]{2,1,0:T(2,128)(2,1)S(1)}, u32[]{:S(2)}, u32[]{:S(2)}) %all-to-all-start) | async-done | bytes 262176 | tf_op jit(solution)/shard_map/all_to_all | solution.py:93
  104.6 0.5 reshape.55
  105.1 48.9 %all-reduce.5.cloned.1.call-done = bf16[32,2048]{1,0:T(8,128)(2,1)} async-done(((bf16[32,2048]{1,0:T(8,128)(2,1)}), bf16[32,2048]{1,0:T(8,128)(2,1)}) %all-reduce.5.cloned.1.call-update) | async-done | bytes 131088 | tf_op jit(solution)/shard_map/psum | solution.py:103
  154.1 4.8 %conditional.3 = (bf16[64,32,32]{0,1,2:T(8,128)(2,1)S(1)}) conditional(s32[]{:T(128)} %convert_element_type.78, () %tuple.19, (bf16[1,32,128,32]{3,1,2,0:T(8,128)(2,1)S(1)}, bf16[32,2048]{1,0:T(8,128)(2,1)}, bf16[2048]{0:T(1024)(128)(2,1)S(1)}, bf16[1,192,2048]{2,1,0:T(8,128)(2,1)}, bf16[1,192,2048]{2,1,0:T(8,128)(2,1)}, ...), branch_computations={%region_9.10_spmd, %region_10.12_spmd} | conditional | flops 76781600 | bytes 13064156 | solution.py:129
  154.1 0.4 copy.69
  154.5 1.2 all_to_all.9
  155.9 0.4 fusion.21
  156.3 0.5 copy.70
  156.8 0.6 copy-done.4
  157.4 1.5 fusion.16
  158.9 0.9 copy.71
  160.0 0.8 reshape.58
  160.8 22.4 %all_to_all.41 = bf16[128,2,512]{2,1,0:T(2,128)(2,1)S(1)} all-to-all(bf16[128,2,512]{2,1,0:T(2,128)(2,1)S(1)} %reshape.58), channel_id=1, replica_groups=mesh['pool'=2,'wide'=64,'narrow'=4] {'pool','wide'}, dimensions={0} | all-to-all | bytes 524288 | tf_op jit(solution)/shard_map/all_to_all | solution.py:134
  183.2 0.5 reshape.59
  184.1 0.7 copy.78
  184.8 40.6 %reduce-scatter.4.cloned.1.call-done = f32[16,32]{1,0:T(8,128)} async-done(((f32[128,32]{1,0:T(8,128)}), f32[16,32]{1,0:T(8,128)}) %reduce-scatter.4.cloned.1.call-update) | async-done | bytes 2064
  225.4 0.8 copy.79
  226.3 0.7 copy.73
  (53 shorter events, 3.1 us)
Async XLA Ops:
  6.5 58.1 %copy-start = (bf16[32,2048]{1,0:T(8,128)(2,1)S(1)}, bf16[32,2048]{1,0:T(8,128)(2,1)}, u32[]{:S(2)}) copy-start(bf16[32,2048]{1,0:T(8,128)(2,1)} %param.25) | copy-start | bytes 393220
  6.5 1.2 copy-start.12
  7.3 1.0 copy-start.5
  7.6 0.7 copy-start.14
  7.7 0.7 copy-start.9
  7.7 0.7 copy-start.11
  7.7 0.7 copy-start.13
  66.9 8.4 %copy-start.8 = (bf16[128,32]{0,1:T(8,128)(2,1)S(1)}, bf16[128,32]{0,1:T(8,128)(2,1)}, u32[]{:S(2)}) copy-start(bf16[128,32]{0,1:T(8,128)(2,1)} %param.24) | copy-start | bytes 24580
  66.9 18.1 %all-to-all-start.1 = ((bf16[128,2,512]{2,1,0:T(2,128)(2,1)}), bf16[128,2,512]{2,1,0:T(2,128)(2,1)S(1)}, u32[]{:S(2)}, u32[]{:S(2)}) async-start(bf16[128,2,512]{2,1,0:T(2,128)(2,1)} %reshape.56), calls=%async_computation.1 | async-start | bytes 524288 | tf_op jit(solution)/shard_map/all_to_all | solution.py:86
  75.8 1.5 copy-start.7
  85.0 19.5 %all-to-all-start = ((bf16[128,2,512]{2,1,0:T(2,128)(2,1)}), bf16[128,2,512]{2,1,0:T(2,128)(2,1)S(1)}, u32[]{:S(2)}, u32[]{:S(2)}) async-start(bf16[128,2,512]{2,1,0:T(2,128)(2,1)} %reshape.54), calls=%async_computation | async-start | bytes 524288 | tf_op jit(solution)/shard_map/all_to_all | solution.py:93
  94.9 59.1 %all-reduce.5.cloned.1.call-start = ((), (), s32[]{:S(2)}) async-start(), calls=%async_computation.4 | async-start | bytes 262144 | tf_op jit(solution)/shard_map/psum | solution.py:103
  97.3 0.8 copy-start.6
  97.9 56.1 %copy-start.2 = (bf16[1,192,2048]{2,1,0:T(8,128)(2,1)S(1)}, bf16[1,192,2048]{2,1,0:T(8,128)(2,1)}, u32[]{:S(2)}) copy-start(bf16[1,192,2048]{2,1,0:T(8,128)(2,1)} %param.31) | copy-start | bytes 2359300
  98.0 127.5 %reduce-scatter.4.cloned.1.call-start = ((), (), s32[]{:S(2)}) async-start(), calls=%async_computation.5 | async-start | bytes 73728
  98.9 55.1 %copy-start.10 = (bf16[2048]{0:T(1024)(128)(2,1)S(1)}, bf16[2048]{0:T(1024)(128)(2,1)}, u32[]{:S(2)}) copy-start(bf16[2048]{0:T(1024)(128)(2,1)} %param.26) | copy-start | bytes 12292
  154.5 1.2 copy-start.1
  154.5 1.4 copy-start.3
  156.2 1.2 copy-start.4
Sparse Core Ops, SparseCore 0:
  98.7 55.3 all-reduce.4
  184.9 40.4 reduce-scatter.3
where the time goes:
time: 234 us
  waiting for transfers between devices  102 us (44%)
  blocking collectives  78.3 us (33%)
  starting transfers between devices  18.6 us (8%)
  local copies, waits for them, and re-layouts  15 us (6%)
  between operations  13.7 us (6%)
  matrix products  3.98 us (2%)
  other arithmetic  2.34 us (1%)
    all_gather x1, blocking collectives, local(): lax.all_gather(heads_local, 'wide', axis=0, tiled=True)  55.9 us
    psum x1, waiting for transfers between devices, local(): lax.psum(arrived_part.astype(jnp.float32).astype(jnp.bfloat16), 'narrow')  48.9 us
    unnamed x3, waiting for transfers between devices  40.6 us
    all_to_all x1, blocking collectives, local(): lax.all_to_all(jnp.concatenate([produced, jnp.zeros_like(produced)], axis...  22.4 us
    all_to_all x1, starting transfers between devices, local(): lax.all_to_all(jnp.concatenate([blank, send_resid], axis=0), ('pool', 'wi...  9.88 us
    all_to_all x1, starting transfers between devices, local(): lax.all_to_all(jnp.concatenate([blank, send_part], axis=0), ('pool', 'wid...  8.42 us
    unnamed x33, local copies, waits for them, and re-layouts  7.79 us
    all_to_all x1, waiting for transfers between devices, local(): lax.all_to_all(jnp.concatenate([blank, send_part], axis=0), ('pool', 'wid...  6.6 us
  transfers between devices with their start and end apart: 4, of which 4 were waited for; matrix products, arithmetic and copies ran while one was open for 3% of the time, Pallas kernels for 0%

commit v1 on v0

v1 whole, which is shorter than its diff:
```python
import functools

import jax
import jax.numpy as jnp
from jax import lax
from jax.experimental import pallas as pl
from jax.experimental.pallas import tpu as pltpu
from jax.sharding import PartitionSpec as P

BF16, F32 = jnp.bfloat16, jnp.float32
NT = (((1,), (1,)), ((), ()))
HIGH = lax.Precision.HIGHEST


def iota(shape, axis):
    return lax.broadcasted_iota(jnp.int32, shape, axis)


def ones_where(mask, dtype=BF16):
    return jnp.where(mask, 1.0, 0.0).astype(dtype)


def send(src, dst, send_sem, recv_sem, device):
    pltpu.make_async_remote_copy(
        src_ref=src,
        dst_ref=dst,
        send_sem=send_sem,
        recv_sem=recv_sem,
        device_id=device,
        device_id_type=pl.DeviceIdType.MESH,
    ).start()


def wait_bytes(ref, sem):
    pltpu.make_async_copy(ref, ref, sem).wait()


def step(
    q_h, nk_h, nv_h, k_h, v_h, len_h, res_h, w_h, gain_h, ids_h, ew_h, gate_h, up_h, down_h,
    out_ref,
    q_v, nk_v, nv_v, k_v, v_v, len_v, res_v, w_v, gain_v, ids_v, ew_v, gate_v, up_v, down_v,
    heads, heads_f, parts, hidden, gu_w, down_w, made, summed, partial, by_z, final,
    load_sem, send_sem, recv_sem,
):
    p = lax.axis_index("pool")
    w = lax.axis_index("wide")
    n = lax.axis_index("narrow")
    z, xc = w // 8, w % 8
    pn = p * 4 + n

    loads = [
        (q_h.at[p], q_v), (k_h.at[p], k_v), (len_h, len_v), (nk_h, nk_v), (nv_h, nv_v), (v_h.at[p], v_v),
        (w_h, w_v), (res_h, res_v), (gain_h, gain_v), (ids_h, ids_v), (ew_h, ew_v),
        (gate_h, gate_v), (up_h, up_v), (down_h, down_v),
    ]
    loads = [pltpu.make_async_copy(s, d, load_sem.at[i]) for i, (s, d) in enumerate(loads)]
    for copy in loads:
        copy.start()

    z_peers = [{"wide": (z + d) % 8 * 8 + xc} for d in range(1, 8)]
    xc_peers = [{"wide": z * 8 + (xc + d) % 8} for d in range(1, 8)]
    n_peers = [{"narrow": (n + d) % 4} for d in range(1, 4)]
    pn_peers = [{"pool": (pn + d) % 8 // 4, "narrow": (pn + d) % 4} for d in range(1, 8)]

    barrier = pltpu.get_barrier_semaphore()
    peers = z_peers + xc_peers + pn_peers
    for peer in peers:
        pl.semaphore_signal(barrier, inc=1, device_id=peer, device_id_type=pl.DeviceIdType.MESH)

    for copy in loads[:6]:
        copy.wait()
    q = q_v[...]
    scale = 128.0**-0.5
    scores = lax.dot_general(q, k_v[...], NT, preferred_element_type=F32) * scale
    nk = jnp.where(p == 0, nk_v[0:1].astype(F32), nk_v[1:2].astype(F32))
    nv = jnp.where(p == 0, nv_v[0:1].astype(F32), nv_v[1:2].astype(F32))
    self_score = jnp.sum(q.astype(F32) * nk, axis=1, keepdims=True) * scale
    valid = iota((16, 512), 1) < len_v[p]
    scores = jnp.where(valid, scores, -1e30)
    peak = jnp.maximum(jnp.max(scores, axis=1, keepdims=True), self_score)
    weights = jnp.where(valid, jnp.exp(scores - peak), 0.0)
    self_weight = jnp.exp(self_score - peak)
    total = jnp.sum(weights, axis=1, keepdims=True) + self_weight
    probs = (weights / total).astype(BF16)
    self_prob = (self_weight / total).astype(BF16).astype(F32)
    mixed = jnp.dot(probs, v_v[...], preferred_element_type=F32) + self_prob * nv
    heads[z, xc] = mixed.astype(BF16)

    def spread_z(buf, phase):
        mine = buf.at[z, xc]
        for peer in z_peers:
            send(mine, mine, send_sem.at[phase], recv_sem.at[phase], peer)

    def spread_xc(buf, phase):
        wait_bytes(buf.at[pl.ds(0, 7), 0], recv_sem.at[phase - 1])
        mine = buf.at[:, xc]
        for peer in xc_peers:
            send(mine, mine, send_sem.at[phase], recv_sem.at[phase], peer)

    def arrive_xc(buf, phase):
        wait_bytes(buf.at[:, pl.ds(0, 7)], recv_sem.at[phase])

    pl.semaphore_wait(barrier, len(peers))
    spread_z(heads, 0)

    for copy in loads[6:]:
        copy.wait()
    gain = gain_v[...].reshape(1, 2048).astype(F32)
    src, dst = iota((256, 256), 0), iota((256, 256), 1)
    perm = ones_where(dst == (src % 32 // 16) * 128 + src // 32 * 16 + src % 16)
    for i, ref in enumerate((gate_v, up_v)):
        for b in range(8):
            cols = slice(b * 256, (b + 1) * 256)
            scaled = (ref[:, cols].astype(F32) * gain[:, cols]).astype(BF16)
            moved = jnp.dot(scaled, perm, preferred_element_type=F32).astype(BF16)
            gu_w[i * 192 : (i + 1) * 192, b * 128 : (b + 1) * 128] = moved[:, :128]
            gu_w[384 + i * 192 : 384 + (i + 1) * 192, b * 128 : (b + 1) * 128] = moved[:, 128:]

    spread_xc(heads, 1)

    perm_t = ones_where(src == (dst % 32 // 16) * 128 + dst // 32 * 16 + dst % 16)
    for b in range(8):
        block = down_v[:, b * 256 : (b + 1) * 256]
        moved = lax.dot_general(perm_t, block, NT, preferred_element_type=F32).astype(BF16)
        down_w[0, b * 128 : (b + 1) * 128] = moved[:128]
        down_w[1, b * 128 : (b + 1) * 128] = moved[128:]
    row, lane = iota((128, 128), 0), iota((128, 128), 1)
    pick_low = (lane < 64) & (row == 2 * lane + p)
    pick_high = (lane >= 64) & (row == 2 * (lane - 64) + p)
    res = res_v[...]
    own_res = jnp.dot(res[0:16], ones_where(pick_low), preferred_element_type=F32) + jnp.dot(
        res[16:32], ones_where(pick_high), preferred_element_type=F32
    )
    ew = ew_v[...]
    share = jnp.sum(jnp.where(ids_v[...] == w, ew, 0.0), axis=0, keepdims=True)
    share = share / jnp.sum(ew, axis=0, keepdims=True)
    share = jnp.dot(
        jnp.broadcast_to(share, (8, 128)), ones_where(pick_low, F32), precision=HIGH, preferred_element_type=F32
    )[0:1]
    out_row, out_lane = iota((16, 128), 0), iota((16, 128), 1)
    first = pn * 16
    out_res = lax.dot_general(ones_where(out_lane == first + out_row), res, NT, preferred_element_type=F32)

    arrive_xc(heads, 1)
    heads_f[...] = heads[...].reshape(1024, 128).astype(F32)
    rows = jnp.concatenate([heads_f[pl.ds(g, 64, stride=16), :].astype(BF16) for g in range(16)], axis=1)
    part = lax.dot_general(w_v[...], rows, NT, preferred_element_type=F32)
    part = jnp.concatenate([part[0:16], part[16:32]], axis=1).astype(BF16)

    parts[n] = part
    for peer in n_peers:
        send(parts.at[n], parts.at[n], send_sem.at[2], recv_sem.at[2], peer)
    wait_bytes(parts.at[pl.ds(0, 3)], recv_sem.at[2])
    own = own_res
    for i in range(4):
        own = own + parts[i].astype(F32)
    hidden[z, xc] = own.astype(BF16)
    spread_z(hidden, 3)
    spread_xc(hidden, 4)
    arrive_xc(hidden, 4)

    hid = hidden[...].reshape(1024, 128)
    both = jnp.dot(gu_w[...], hid, preferred_element_type=F32)
    hid_f = hid.astype(F32)
    square = jnp.sum(hid_f * hid_f, axis=0, keepdims=True)
    square = square + pltpu.roll(square, 64, 1)
    inv = lax.rsqrt(square * (1.0 / 2048) + 1e-6)
    both = (both[0:384] + pltpu.roll(both[384:768], 64, 1)) * inv
    gate_vals, up_vals = both[0:192], both[192:384]
    act = gate_vals / (1.0 + jnp.exp(-gate_vals)) * up_vals * share
    act_low, act_high = act.astype(BF16), pltpu.roll(act, 64, 1).astype(BF16)
    output = jnp.dot(down_w[0], act_low, preferred_element_type=F32) + jnp.dot(
        down_w[1], act_high, preferred_element_type=F32
    )
    made[...] = output.astype(BF16).reshape(8, 8, 16, 128)

    for d, peer in zip(range(1, 8), xc_peers):
        send(made.at[:, (xc + d) % 8], partial.at[xc], send_sem.at[5], recv_sem.at[5], peer)
    partial[xc] = made[:, xc]
    wait_bytes(partial.at[pl.ds(0, 7)], recv_sem.at[5])
    acc = partial[0].astype(F32)
    for i in range(1, 8):
        acc = acc + partial[i].astype(F32)
    summed[...] = acc.astype(BF16)
    for d, peer in zip(range(1, 8), z_peers):
        send(summed.at[(z + d) % 8], by_z.at[z], send_sem.at[6], recv_sem.at[6], peer)
    by_z[z] = summed[z]
    wait_bytes(by_z.at[pl.ds(0, 7)], recv_sem.at[6])
    acc = part.astype(F32)
    for i in range(8):
        acc = acc + by_z[i].astype(F32)
    final[pn] = acc.astype(BF16)
    for peer in pn_peers:
        send(final.at[pn], final.at[pn], send_sem.at[7], recv_sem.at[7], peer)
    wait_bytes(final.at[pl.ds(0, 7)], recv_sem.at[7])
    even, odd = final[0].astype(F32), final[4].astype(F32)
    for i in range(1, 4):
        even, odd = even + final[i].astype(F32), odd + final[4 + i].astype(F32)
    low = out_lane < 64
    table = jnp.concatenate(
        [jnp.where(low, even, pltpu.roll(odd, 64, 1)), jnp.where(low, pltpu.roll(even, 64, 1), odd)], axis=0
    )
    chosen = jnp.where(low, 2 * out_lane, 2 * (out_lane - 64) + 1) == first + out_row
    out = lax.dot_general(ones_where(chosen, F32), table, NT, precision=HIGH, preferred_element_type=F32)
    out_ref[...] = (out + out_res).astype(BF16)

    for phase, ref in (
        (0, heads.at[pl.ds(0, 7), 0]),
        (1, heads.at[:, pl.ds(0, 7)]),
        (2, parts.at[pl.ds(0, 3)]),
        (3, hidden.at[pl.ds(0, 7), 0]),
        (4, hidden.at[:, pl.ds(0, 7)]),
        (5, partial.at[pl.ds(0, 7)]),
        (6, by_z.at[pl.ds(0, 7)]),
        (7, final.at[pl.ds(0, 7)]),
    ):
        wait_bytes(ref, send_sem.at[phase])


def local(
    queries, new_keys, new_values, key_cache, value_cache, lengths, residual, out_weight, norm_gain,
    expert_ids, expert_weights, gate_proj, up_proj, down_proj,
):
    args = (
        queries, new_keys[:, 0, :], new_values[:, 0, :], key_cache[:, :, 0, :], value_cache[:, :, 0, :], lengths,
        residual.T, out_weight, norm_gain, expert_ids.T, expert_weights.T, gate_proj[0], up_proj[0], down_proj[0],
    )
    held = [pltpu.VMEM(a.shape, a.dtype) for a in args]
    for i in (0, 3, 4):
        held[i] = pltpu.VMEM(args[i].shape[1:], BF16)
    held[5] = pltpu.SMEM((2,), jnp.int32)
    tiles = lambda *lead: pltpu.VMEM((*lead, 16, 128), BF16)
    return pl.pallas_call(
        step,
        out_shape=jax.ShapeDtypeStruct((16, 32), BF16),
        in_specs=[pl.BlockSpec(memory_space=pl.ANY)] * len(args),
        out_specs=pl.BlockSpec(memory_space=pltpu.VMEM),
        scratch_shapes=held
        + [
            tiles(8, 8), pltpu.VMEM((1024, 128), F32), tiles(4), tiles(8, 8),
            pltpu.VMEM((768, 1024), BF16), pltpu.VMEM((2, 1024, 192), BF16),
            tiles(8, 8), tiles(8), tiles(8, 8), tiles(8), tiles(8),
            pltpu.SemaphoreType.DMA((14,)), pltpu.SemaphoreType.DMA((8,)), pltpu.SemaphoreType.DMA((8,)),
        ],
        compiler_params=pltpu.CompilerParams(
            collective_id=0, has_side_effects=True, vmem_limit_bytes=56 * 1024 * 1024
        ),
    )(*args)


def solution(mesh):
    in_specs = (
        P("wide", "narrow", None),
        P("wide", "narrow", None),
        P("wide", "narrow", None),
        P("wide", None, "narrow", None),
        P("wide", None, "narrow", None),
        P("wide"),
        P(None, "wide"),
        P("wide", "narrow"),
        P(),
        P(),
        P(),
        P("wide", "narrow", None),
        P("wide", "narrow", None),
        P("wide", "narrow", None),
    )
    return jax.shard_map(
        local, mesh=mesh, in_specs=in_specs, out_specs=P(("pool", "narrow"), "wide"), check_vma=False
    )
```

time: 234 us -> 56.1 us (0.24)
  the two profiles are of different devices: /device:TPU:12 before, /device:TPU:1 now
where the time goes in v1:
time: 56.1 us; the launch traced here: 55.9 us
  Pallas kernels  54.6 us (97%)
  local copies, waits for them, and re-layouts  1.28 us (2%)
    pallas_call x1, Pallas kernels, local(): pl.pallas_call(step, out_shape=jax.ShapeDtypeStruct((16, 32), BF16), in_s...  54.6 us
    unnamed x1, local copies, waits for them, and re-layouts  1.28 us

profile of v1, /device:TPU:1, one launch (start us, length us, event | category | flops | bytes accessed | tf_op | source)
XLA Modules:
  0.0 55.9 jit_solution(4313308712466686402)
XLA Ops:
  0.0 54.6 %shard_map.136 = bf16[16,32]{1,0:T(8,128)(2,1)} custom-call(bf16[2,16,128]{2,1,0:T(8,128)(2,1)} %q_h.1, bf16[2,128]{1,0:T(2,128)(2,1)} %bitcast.18, bf16[2,128]{1,0:T(2,128)(2,1)} %bitcast.19, bf16[2,512,128]{2,1,0:T(8,128)(2,1)} %bitcast.13, bf16[2,512,128]{2,1,0:T(8,128)(2,1)} %bitcast.14, s32[2]{0:T(128)} %len_h.1, bf16[32,128]{1,0:T(8,128)(2,1)} %bitcast.15, ...), custom_call_target="tpu_custom_call" | custom-call | tf_op jit(solution)/shard_map/pallas_call | solution.py:233
  54.6 1.3 %copy.16 = bf16[16,32]{1,0:T(8,128)(2,1)} copy(bf16[16,32]{1,0:T(8,128)(2,1)} %shard_map.136) | data formatting | bytes 2048

commit v2 on v1

v2 whole, which is shorter than its diff:
```python
import functools

import jax
import jax.numpy as jnp
from jax import lax
from jax.experimental import pallas as pl
from jax.experimental.pallas import tpu as pltpu
from jax.sharding import PartitionSpec as P

BF16, F32 = jnp.bfloat16, jnp.float32
NT = (((1,), (1,)), ((), ()))
HIGH = lax.Precision.HIGHEST


def iota(shape, axis):
    return lax.broadcasted_iota(jnp.int32, shape, axis)


def ones_where(mask, dtype=BF16):
    return jnp.where(mask, 1.0, 0.0).astype(dtype)


def send(src, dst, send_sem, recv_sem, device):
    pltpu.make_async_remote_copy(
        src_ref=src,
        dst_ref=dst,
        send_sem=send_sem,
        recv_sem=recv_sem,
        device_id=device,
        device_id_type=pl.DeviceIdType.MESH,
    ).start()


def wait_bytes(ref, sem):
    pltpu.make_async_copy(ref, ref, sem).wait()


FAR, NEAR = (4, 3, 5, 2, 6, 1, 7), (1, 7, 2, 6, 3, 5, 4)


def far_offset(i):
    return 4 + (2 * (i % 2) - 1) * ((i + 1) // 2)


def step(
    k_h, q_h, len_h, nk_h, nv_h, v_h, w_h, res_h, gain_h, ids_h, ew_h, gate_h, up_h, down_h,
    out_ref,
    k_v, q_v, len_v, nk_v, nv_v, v_v, w_v, res_v, gain_v, ids_v, ew_v, gate_v, up_v, down_v,
    heads, heads_f, parts, hidden, gu_w, down_w, both, made, partial, pieces, final,
    load_sem, send_sem, recv_sem,
):
    p = lax.axis_index("pool")
    w = lax.axis_index("wide")
    n = lax.axis_index("narrow")
    z, xc = w // 8, w % 8
    pn = p * 4 + n

    loads = [
        (k_h.at[p], k_v), (q_h.at[p], q_v), (len_h, len_v), (nk_h, nk_v), (nv_h, nv_v), (v_h.at[p], v_v),
        (w_h, w_v), (res_h, res_v), (gain_h, gain_v), (ids_h, ids_v), (ew_h, ew_v),
        (gate_h, gate_v), (up_h, up_v), (down_h, down_v),
    ]
    loads = [pltpu.make_async_copy(s, d, load_sem.at[i]) for i, (s, d) in enumerate(loads)]
    for copy in loads[:6]:
        copy.start()

    def at_z(dz):
        return (z + dz) % 8

    def wide_peer(dz, dxc):
        return {"wide": at_z(dz) * 8 + (xc + dxc) % 8}

    def zn_peer(dz, dn):
        return {"wide": at_z(dz) * 8 + xc, "narrow": (n + dn) % 4}

    def zpn_peer(dz, dpn):
        return {"pool": (pn + dpn) % 8 // 4, "wide": at_z(dz) * 8 + xc, "narrow": (pn + dpn) % 4}

    barrier = pltpu.get_barrier_semaphore()
    greeted = [wide_peer(d, 0) for d in FAR] + [zn_peer(0, d) for d in (2, 1, 3)]
    greeted += [wide_peer(0, d) for d in FAR] + [{"pool": 1 - p}]
    for peer in greeted:
        pl.semaphore_signal(barrier, inc=1, device_id=peer, device_id_type=pl.DeviceIdType.MESH)
    for copy in loads[6:]:
        copy.start()

    loads[0].wait()
    loads[1].wait()
    q = q_v[...]
    scale = 128.0**-0.5
    scores = lax.dot_general(q, k_v[...], NT, preferred_element_type=F32) * scale
    for copy in loads[2:6]:
        copy.wait()
    nk = jnp.where(p == 0, nk_v[0:1].astype(F32), nk_v[1:2].astype(F32))
    nv = jnp.where(p == 0, nv_v[0:1].astype(F32), nv_v[1:2].astype(F32))
    self_score = jnp.sum(q.astype(F32) * nk, axis=1, keepdims=True) * scale
    valid = iota((16, 512), 1) < len_v[p]
    scores = jnp.where(valid, scores, -1e30)
    peak = jnp.maximum(jnp.max(scores, axis=1, keepdims=True), self_score)
    weights = jnp.where(valid, jnp.exp(scores - peak), 0.0)
    self_weight = jnp.exp(self_score - peak)
    total = jnp.sum(weights, axis=1, keepdims=True) + self_weight
    probs = (weights / total).astype(BF16)
    self_prob = (self_weight / total).astype(BF16).astype(F32)
    mixed = jnp.dot(probs, v_v[...], preferred_element_type=F32) + self_prob * nv
    heads[z, xc] = mixed.astype(BF16)

    def fan_out(source, send_index, recv_index):
        @pl.loop(0, 7)
        def _(i):
            send(source, source, send_sem.at[send_index], recv_sem.at[recv_index], wide_peer(0, far_offset(i)))

    pl.semaphore_wait(barrier, len(greeted))
    for d in FAR:
        send(heads.at[z, xc], heads.at[z, xc], send_sem.at[0], recv_sem.at[d], wide_peer(d, 0))
    fan_out(heads.at[z, xc], 1, 0)

    for copy in loads[6:]:
        copy.wait()
    gain = gain_v[...].reshape(1, 2048).astype(F32)
    src, dst = iota((256, 256), 0), iota((256, 256), 1)
    perm = ones_where(dst == (src % 32 // 16) * 128 + src // 32 * 16 + src % 16)
    for i, ref in enumerate((gate_v, up_v)):
        for b in range(8):
            cols = slice(b * 256, (b + 1) * 256)
            scaled = (ref[:, cols].astype(F32) * gain[:, cols]).astype(BF16)
            moved = jnp.dot(scaled, perm, preferred_element_type=F32).astype(BF16)
            gu_w[i * 192 : (i + 1) * 192, b * 128 : (b + 1) * 128] = moved[:, :128]
            gu_w[384 + i * 192 : 384 + (i + 1) * 192, b * 128 : (b + 1) * 128] = moved[:, 128:]

    for d in NEAR:
        tile = heads.at[at_z(8 - d), xc]
        wait_bytes(tile, recv_sem.at[d])
        fan_out(tile, 1, 0)

    perm_t = ones_where(src == (dst % 32 // 16) * 128 + dst // 32 * 16 + dst % 16)
    for b in range(8):
        block = down_v[:, b * 256 : (b + 1) * 256]
        moved = lax.dot_general(perm_t, block, NT, preferred_element_type=F32).astype(BF16)
        down_w[0, b * 128 : (b + 1) * 128] = moved[:128]
        down_w[1, b * 128 : (b + 1) * 128] = moved[128:]
    row, lane = iota((128, 128), 0), iota((128, 128), 1)
    pick_low = (lane < 64) & (row == 2 * lane + p)
    pick_high = (lane >= 64) & (row == 2 * (lane - 64) + p)
    res = res_v[...]
    own_res = jnp.dot(res[0:16], ones_where(pick_low), preferred_element_type=F32) + jnp.dot(
        res[16:32], ones_where(pick_high), preferred_element_type=F32
    )
    own_res = jnp.where(n == 0, own_res, 0.0)
    ew = ew_v[...]
    share = jnp.sum(jnp.where(ids_v[...] == w, ew, 0.0), axis=0, keepdims=True)
    share = share / jnp.sum(ew, axis=0, keepdims=True)
    share = jnp.dot(
        jnp.broadcast_to(share, (8, 128)), ones_where(pick_low, F32), precision=HIGH, preferred_element_type=F32
    )[0:1]
    out_row, out_lane = iota((16, 128), 0), iota((16, 128), 1)
    out_res = lax.dot_general(ones_where(out_lane == pn * 16 + out_row), res, NT, preferred_element_type=F32)

    wait_bytes(heads.at[:, pl.ds(0, 7)], recv_sem.at[0])
    heads_f[...] = heads[...].reshape(1024, 128).astype(F32)
    rows = jnp.concatenate([heads_f[pl.ds(g, 64, stride=16), :].astype(BF16) for g in range(16)], axis=1)
    part = lax.dot_general(w_v[...], rows, NT, preferred_element_type=F32)
    part = jnp.concatenate([part[0:16], part[16:32]], axis=1).astype(BF16).astype(F32)

    parts[z * 4 + n] = (part + own_res).astype(BF16)
    for dn in (2, 1, 3, 0):
        for dz in FAR + (0,) if dn else FAR:
            send(parts.at[z * 4 + n], parts.at[z * 4 + n], send_sem.at[2], recv_sem.at[8 + dz], zn_peer(dz, dn))
    for dz in (0,) + NEAR:
        from_z = at_z(8 - dz)
        wait_bytes(parts.at[pl.ds(0, 4 if dz else 3)], recv_sem.at[8 + dz])
        hid = parts[from_z * 4].astype(F32)
        for i in range(1, 4):
            hid = hid + parts[from_z * 4 + i].astype(F32)
        hidden[from_z, xc] = hid.astype(BF16)
        fan_out(hidden.at[from_z, xc], 3, 16 + dz)

    square = jnp.zeros((1, 128), F32)
    for group in ((0,), (1, 7), (2, 6), (3, 5), (4,)):
        tiles, blocks = [], []
        for dz in group:
            from_z = at_z(8 - dz)
            wait_bytes(hidden.at[from_z, pl.ds(0, 7)], recv_sem.at[16 + dz])
            tiles.append(hidden[from_z].reshape(128, 128))
            blocks.append(gu_w[:, pl.ds(pl.multiple_of(from_z * 128, 128), 128)])
        tile = jnp.concatenate(tiles, axis=0)
        term = jnp.dot(jnp.concatenate(blocks, axis=1), tile, preferred_element_type=F32)
        both[...] = term if group == (0,) else both[...] + term
        tile = tile.astype(F32)
        square = square + jnp.sum(tile * tile, axis=0, keepdims=True)
    square = square + pltpu.roll(square, 64, 1)
    inv = lax.rsqrt(square * (1.0 / 2048) + 1e-6)
    act = (both[0:384] + pltpu.roll(both[384:768], 64, 1)) * inv
    gate_vals, up_vals = act[0:192], act[192:384]
    act = gate_vals / (1.0 + jnp.exp(-gate_vals)) * up_vals * share
    act_low, act_high = act.astype(BF16), pltpu.roll(act, 64, 1).astype(BF16)

    for dz in FAR + (0,):
        to_z = at_z(dz)
        rows_w = pl.ds(pl.multiple_of(to_z * 128, 128), 128)
        output = jnp.dot(down_w[0, rows_w], act_low, preferred_element_type=F32) + jnp.dot(
            down_w[1, rows_w], act_high, preferred_element_type=F32
        )
        made[to_z] = output.astype(BF16).reshape(8, 16, 128)

        @pl.loop(0, 7)
        def _(i):
            d = far_offset(i)
            send(
                made.at[to_z, (xc + d) % 8], partial.at[to_z, xc], send_sem.at[4], recv_sem.at[24 + dz],
                wide_peer(0, d),
            )

        partial[to_z, xc] = made[to_z, xc]

    low = out_lane < 64
    repeat = ones_where(iota((128, 16), 0) // 8 == iota((128, 16), 1))
    same_row = lane % 8 == row % 8
    piece_of = ones_where((out_lane // 64 == out_row % 2) & (out_lane % 64 // 8 == out_row // 2))
    for dz in FAR + (0,):
        to_z = at_z(dz)
        wait_bytes(partial.at[to_z, pl.ds(0, 7)], recv_sem.at[24 + dz])
        acc = partial[to_z, 0].astype(F32)
        for i in range(1, 8):
            acc = acc + partial[to_z, i].astype(F32)
        if dz == 0:
            acc = acc + part
        spread = jnp.dot(repeat, acc.astype(BF16), preferred_element_type=F32)
        spread = jnp.where(same_row, spread, 0.0).astype(BF16)
        piece = lax.dot_general(piece_of, spread, NT, preferred_element_type=F32)
        pieces[to_z] = piece.reshape(8, 2, 128)

        @pl.loop(0, 7)
        def _(i):
            d = far_offset(i)
            send(pieces.at[to_z, (pn + d) % 8], final.at[z * 8 + pn], send_sem.at[5], recv_sem.at[32], zpn_peer(dz, d))

        if dz:
            send(pieces.at[to_z, pn], final.at[z * 8 + pn], send_sem.at[5], recv_sem.at[32], zpn_peer(dz, 0))
        else:
            final[z * 8 + pn] = pieces[z, pn]

    wait_bytes(final.at[pl.ds(0, 63)], recv_sem.at[32])
    acc = final[0:8]
    for i in range(1, 8):
        acc = acc + final[i * 8 : (i + 1) * 8]
    even, odd = acc[0] + acc[1] + acc[2] + acc[3], acc[4] + acc[5] + acc[6] + acc[7]
    chosen, is_even = out_row // 2 == out_lane % 8, out_row % 2 == 0
    table = jnp.concatenate(
        [jnp.where(chosen, jnp.where(is_even, even[h : h + 1], odd[h : h + 1]), 0.0) for h in range(2)], axis=1
    )
    place = ones_where(iota((256, 32), 0) // 8 == iota((256, 32), 1), F32)
    out = jnp.dot(table, place, precision=HIGH, preferred_element_type=F32)
    out_ref[...] = (out + out_res).astype(BF16)

    for index, ref in (
        (0, heads.at[pl.ds(0, 7), 0]),
        (1, heads.at[:, pl.ds(0, 7)]),
        (2, parts.at[pl.ds(0, 31)]),
        (3, hidden.at[:, pl.ds(0, 7)]),
        (4, partial.at[:, pl.ds(0, 7)]),
        (5, final.at[pl.ds(0, 63)]),
    ):
        wait_bytes(ref, send_sem.at[index])


def local(
    queries, new_keys, new_values, key_cache, value_cache, lengths, residual, out_weight, norm_gain,
    expert_ids, expert_weights, gate_proj, up_proj, down_proj,
):
    args = (
        key_cache[:, :, 0, :], queries, lengths, new_keys[:, 0, :], new_values[:, 0, :], value_cache[:, :, 0, :],
        out_weight, residual.T, norm_gain, expert_ids.T, expert_weights.T, gate_proj[0], up_proj[0], down_proj[0],
    )
    args = [pltpu.with_memory_space_constraint(a, pltpu.HBM) for a in args]
    held = [pltpu.VMEM(a.shape, a.dtype) for a in args]
    for i in (0, 1, 5):
        held[i] = pltpu.VMEM(args[i].shape[1:], BF16)
    held[2] = pltpu.SMEM((2,), jnp.int32)
    tiles = lambda *lead: pltpu.VMEM((*lead, 16, 128), BF16)
    return pl.pallas_call(
        step,
        out_shape=pltpu.VMEM((16, 32), BF16),
        in_specs=[pl.BlockSpec(memory_space=pl.ANY)] * len(args),
        out_specs=pl.BlockSpec(memory_space=pltpu.VMEM),
        scratch_shapes=held
        + [
            tiles(8, 8), pltpu.VMEM((1024, 128), F32), tiles(32), tiles(8, 8),
            pltpu.VMEM((768, 1024), BF16), pltpu.VMEM((2, 1024, 192), BF16), pltpu.VMEM((768, 128), F32),
            tiles(8, 8), tiles(8, 8), pltpu.VMEM((8, 8, 2, 128), F32), pltpu.VMEM((64, 2, 128), F32),
            pltpu.SemaphoreType.DMA((14,)), pltpu.SemaphoreType.DMA((6,)), pltpu.SemaphoreType.DMA((33,)),
        ],
        compiler_params=pltpu.CompilerParams(
            collective_id=0, has_side_effects=True, vmem_limit_bytes=32 * 1024 * 1024
        ),
    )(*args)


def solution(mesh):
    in_specs = (
        P("wide", "narrow", None),
        P("wide", "narrow", None),
        P("wide", "narrow", None),
        P("wide", None, "narrow", None),
        P("wide", None, "narrow", None),
        P("wide"),
        P(None, "wide"),
        P("wide", "narrow"),
        P(),
        P(),
        P(),
        P("wide", "narrow", None),
        P("wide", "narrow", None),
        P("wide", "narrow", None),
    )
    return jax.shard_map(
        local, mesh=mesh, in_specs=in_specs, out_specs=P(("pool", "narrow"), "wide"), check_vma=False
    )
```

time: 56.1 us -> 48.9 us (0.87)
  Pallas kernels: 54.6 us -> 48.1 us
  local copies, waits for them, and re-layouts: 1.28 us -> 0.6 us
    pallas_call x1, Pallas kernels: 54.6 us -> 48.1 us  [local(): pl.pallas_call(step, out_shape=pltpu.VMEM((16, 32), BF16), in_specs=[pl.B...]
    unnamed x1, local copies, waits for them, and re-layouts: 1.28 us -> 0.6 us
where the time goes in v2:
time: 48.9 us; the launch traced here: 48.7 us
  Pallas kernels  48.1 us (98%)
  local copies, waits for them, and re-layouts  0.6 us (1%)
    pallas_call x1, Pallas kernels, local(): pl.pallas_call(step, out_shape=pltpu.VMEM((16, 32), BF16), in_specs=[pl.B...  48.1 us

profile of v2, /device:TPU:1, one launch (start us, length us, event | category | flops | bytes accessed | tf_op | source)
XLA Modules:
  0.0 48.7 jit_solution(6311105201740754920)
XLA Ops:
  0.0 48.1 %shard_map.136 = bf16[16,32]{1,0:T(8,128)(2,1)S(1)} custom-call(bf16[2,512,128]{2,1,0:T(8,128)(2,1)} %bitcast.13, bf16[2,16,128]{2,1,0:T(8,128)(2,1)} %q_h.1, s32[2]{0:T(128)} %len_h.1, bf16[2,128]{1,0:T(2,128)(2,1)} %bitcast.18, bf16[2,128]{1,0:T(2,128)(2,1)} %bitcast.19, bf16[2,512,128]{2,1,0:T(8,128)(2,1)} %bitcast.14, bf16[32,2048]{1,0:T(8,128)(2,1)} %w_h.1, ...), custom_call_target="tpu_custom_call" | custom-call | tf_op jit(solution)/shard_map/pallas_call | solution.py:281
  48.1 0.6 %copy.16 = bf16[16,32]{1,0:T(8,128)(2,1)} copy(bf16[16,32]{1,0:T(8,128)(2,1)S(1)} %shard_map.136) | data formatting | bytes 2048

commit v3 on v2

--- a/solution.py
+++ b/solution.py
@@ -106,8 +106,7 @@
     heads[z, xc] = mixed.astype(BF16)
 
     def fan_out(source, send_index, recv_index):
-        @pl.loop(0, 7)
-        def _(i):
+        for i in range(7):
             send(source, source, send_sem.at[send_index], recv_sem.at[recv_index], wide_peer(0, far_offset(i)))
 
     pl.semaphore_wait(barrier, len(greeted))
@@ -203,8 +202,7 @@
         )
         made[to_z] = output.astype(BF16).reshape(8, 16, 128)
 
-        @pl.loop(0, 7)
-        def _(i):
+        for i in range(7):
             d = far_offset(i)
             send(
                 made.at[to_z, (xc + d) % 8], partial.at[to_z, xc], send_sem.at[4], recv_sem.at[24 + dz],
@@ -230,8 +228,7 @@
         piece = lax.dot_general(piece_of, spread, NT, preferred_element_type=F32)
         pieces[to_z] = piece.reshape(8, 2, 128)
 
-        @pl.loop(0, 7)
-        def _(i):
+        for i in range(7):
             d = far_offset(i)
             send(pieces.at[to_z, (pn + d) % 8], final.at[z * 8 + pn], send_sem.at[5], recv_sem.at[32], zpn_peer(dz, d))
 

time: 48.9 us -> 48.7 us (level)
  no operation moved by 1% of the time
where the time goes in v3:
time: 48.7 us; the launch traced here: 48.6 us
  Pallas kernels  48 us (99%)
  local copies, waits for them, and re-layouts  0.6 us (1%)
    pallas_call x1, Pallas kernels, local(): pl.pallas_call(step, out_shape=pltpu.VMEM((16, 32), BF16), in_specs=[pl.B...  48 us

profile of v3, /device:TPU:1, one launch (start us, length us, event | category | flops | bytes accessed | tf_op | source)
XLA Modules:
  0.0 48.6 jit_solution(9564916286396132872)
XLA Ops:
  0.0 48.0 %shard_map.136 = bf16[16,32]{1,0:T(8,128)(2,1)S(1)} custom-call(bf16[2,512,128]{2,1,0:T(8,128)(2,1)} %bitcast.13, bf16[2,16,128]{2,1,0:T(8,128)(2,1)} %q_h.1, s32[2]{0:T(128)} %len_h.1, bf16[2,128]{1,0:T(2,128)(2,1)} %bitcast.18, bf16[2,128]{1,0:T(2,128)(2,1)} %bitcast.19, bf16[2,512,128]{2,1,0:T(8,128)(2,1)} %bitcast.14, bf16[32,2048]{1,0:T(8,128)(2,1)} %w_h.1, ...), custom_call_target="tpu_custom_call" | custom-call | tf_op jit(solution)/shard_map/pallas_call | solution.py:278
  48.0 0.6 %copy.16 = bf16[16,32]{1,0:T(8,128)(2,1)} copy(bf16[16,32]{1,0:T(8,128)(2,1)S(1)} %shard_map.136) | data formatting | bytes 2048
